TPU v7x, 256 devices: a whole 4x4x8 slice. The times are simulated.
256 devices in a mesh: rows: 64 (over z, y, core), cols: 4 (over x).
Axes of the slice: x: 4, y: 4, z: 8, core: 2. Of those that a mesh axis runs over, the one named last changes fastest.
Arguments:
- points: float32 [65536, 1024], P('rows', 'cols'), may hold values from -6 to 6
- pivots: int32 [2, 512], replicated, may hold values from 0 to 65535, as said below
- targets: float32 [65536, 256], P('rows', 'cols'), may hold values from -6 to 6
Outputs:
- factor: float32 [65536, 1024], P(('rows', 'cols'))
- projection: float32 [1024, 256], P(None, 'cols')
Inputs may be any that keep to these rules, and one draw needn't show every extreme that they name: All 1024 indices of both blocks are distinct. The points of one index of rows (an aligned run of 1024 indices) hold at most 64 pivots of the two blocks together, and in every draw some index of rows holds exactly 64.
All inputs are finite; a program needn't handle non-finite values.
Results may differ from a plain program's by a relative error of at most 0.0003.
Values sent between devices are 32-bit elements; how exact they have to be, the bound alone decides.
A program may use at most 64 MiB of HBM per device.

v0:
```python
import math
import jax
import jax.numpy as jnp
from jax import lax
from jax.sharding import Mesh
from jax.sharding import PartitionSpec as P

E = 1024
ROWS = ("rows_0", "rows_1", "rows_2")
ROWS_COLS = ("rows_0", "rows_1", "rows_2", "cols")
RIDGE = 0.001


def in_blocks(value, dim, count):
    before, after = (value.shape[:dim], value.shape[dim + 1 :])
    return jnp.moveaxis(value.reshape(*before, count, -1, *after), dim, 0)


def summed_on_arrival(value, axis, dim):
    count = lax.axis_size(axis)
    blocks = lax.all_to_all(in_blocks(value, dim, count), axis, 0, 0, tiled=True)
    return jnp.sum(blocks, axis=0)


def sum_by_axis(value, axes, dim):
    far, near = axes
    blocks = in_blocks(value, dim, lax.axis_size(far))
    nearer = summed_on_arrival(blocks, near, dim + 1)
    arrived = lax.all_to_all(nearer, far, split_axis=0, concat_axis=0, tiled=True)
    return arrived.sum(axis=0)


def padded_to(lines, count):
    spare = -lines.shape[0] % count
    if not spare:
        return lines
    return jnp.concatenate([lines, jnp.zeros((spare, *lines.shape[1:]), lines.dtype)])


def copy_for_each(value, axis):
    copies = jnp.broadcast_to(value, (lax.axis_size(axis), *value.shape))
    return lax.all_to_all(copies, axis, split_axis=0, concat_axis=0, tiled=True)


def in_order(blocks, dim):
    blocks = jnp.moveaxis(blocks, 0, dim)
    lengths = blocks.shape
    return blocks.reshape(*lengths[:dim], lengths[dim] * lengths[dim + 1], *lengths[dim + 2 :])


def gather_axes(value, axes, dim):
    far, near = axes
    leading = copy_for_each(value, far)
    blocks = jnp.swapaxes(copy_for_each(leading, near), 0, 1)
    return in_order(blocks.reshape(-1, *value.shape), dim)


def sum_by_parts(value, axes):
    lines = value.reshape(-1, value.shape[-1])
    own = sum_by_axis(padded_to(lines, lax.axis_size(axes[0]) * lax.axis_size(axes[1])), axes, 0)
    whole = gather_axes(own, axes, 0)
    return whole[: len(lines)].reshape(value.shape)


def right_side_solve(low, values):
    return lax.linalg.triangular_solve(low, values, left_side=False, lower=True, transpose_a=True)


def shards(points, pivots, targets):
    highest = lax.Precision.HIGHEST
    rows_dev = points.shape[0]
    nrows = lax.axis_size(ROWS)
    row_me = lax.axis_index(ROWS)
    block = pivots.shape[1]
    flat = pivots.reshape(-1)
    owner = flat // rows_dev
    inside = flat - owner * rows_dev
    mine = owner == row_me
    picked = jnp.where(mine[:, None], points[inside], 0.0)
    pivot_part = sum_by_parts(picked, (("rows_0", "rows_1"), "rows_2"))
    own_rows = lax.all_to_all(points, "cols", split_axis=0, concat_axis=1, tiled=True)
    pivot_full = lax.all_gather(pivot_part, "cols", axis=1, tiled=True)
    own_norms = jnp.sum(own_rows * own_rows, axis=1)
    full_norms = jnp.sum(pivot_full * pivot_full, axis=1)
    cross = jnp.dot(own_rows, pivot_full.T, precision=highest, preferred_element_type=jnp.float32)
    dist = own_norms[:, None] + full_norms[None, :] - 2.0 * cross
    kern = jnp.exp(-dist / (2.0 * E))
    first = kern[:, :block]
    second = kern[:, block:]
    identity = jnp.eye(block, dtype=jnp.float32)
    every_norms = jnp.sum(pivot_full * pivot_full, axis=1)
    pivot_cross = jnp.dot(
        pivot_full, pivot_full.T, precision=highest, preferred_element_type=jnp.float32
    )
    pivot_kern = jnp.exp(
        -(every_norms[:, None] + every_norms[None, :] - 2.0 * pivot_cross) / (2.0 * E)
    )
    low_one = jnp.linalg.cholesky(pivot_kern[:block, :block] + RIDGE * identity)
    factor_one = right_side_solve(low_one, first)
    crossed = right_side_solve(low_one, pivot_kern[block:, :block])
    second_pivot = pivot_kern[block:, block:]
    resid = second - jnp.dot(
        factor_one, crossed.T, precision=highest, preferred_element_type=jnp.float32
    )
    schur = second_pivot - jnp.dot(
        crossed, crossed.T, precision=highest, preferred_element_type=jnp.float32
    )
    low_two = jnp.linalg.cholesky(schur + RIDGE * identity)
    second_lower_matrix = right_side_solve(low_two, resid)
    factor = jnp.concatenate([factor_one, second_lower_matrix], axis=1)
    scaling = 1.0 / math.sqrt(rows_dev * nrows)
    summed = lax.dot_general(
        lax.all_gather(factor, "cols", axis=0, tiled=True),
        targets,
        (((0,), (0,)), ((), ())),
        precision=highest,
        preferred_element_type=jnp.float32,
    )
    projection = sum_by_parts(summed, (("rows_0", "rows_1"), "rows_2")) * scaling
    return (factor, projection)


def solution(mesh):
    finer = Mesh(
        mesh.devices.reshape(8, 4, 2, mesh.shape["cols"]), ("rows_0", "rows_1", "rows_2", "cols")
    )
    placed = (P(ROWS, "cols"), P(), P(ROWS, "cols"))
    return jax.shard_map(
        shards,
        mesh=finer,
        in_specs=placed,
        out_specs=(P(ROWS_COLS, None), P(None, "cols")),
        check_vma=False,
    )
```

profile of v0, /device:TPU:1, one launch (start us, length us, event | category | flops | bytes accessed | tf_op | source)
XLA Modules:
  0.0 562.3 jit_solution(10327082064744761221)
XLA Ops:
  9.0 4.7 gather_fusion
  14.8 6.8 %all-to-all-start = ((f32[2,32,16,256]{3,2,1,0:T(8,128)}), f32[2,32,16,256]{3,2,1,0:T(8,128)S(1)}, u32[]{:S(2)}, u32[]{:S(2)}) async-start(f32[2,32,16,256]{3,2,1,0:T(8,128)} %fusion.7), calls=%async_computation | async-start | bytes 2097152 | tf_op jit(solution)/shard_map/all_to_all | solution.py:21
  21.6 1.7 all-to-all-done
  23.5 25.9 %all_to_all.63 = f32[32,16,256]{2,1,0:T(8,128)S(1)} all-to-all(f32[32,16,256]{2,1,0:T(8,128)S(1)} %reduce_sum.58), channel_id=1, replica_groups=mesh['rows_0'=8,'rows_1'=4,'rows_2'=2,'cols'=4] {'rows_0','rows_1'}, dimensions={0} | all-to-all | bytes 1048576 | tf_op jit(solution)/shard_map/all_to_all | solution.py:29
  49.5 20.1 %all_to_all.59 = f32[32,16,256]{2,1,0:T(8,128)S(1)} all-to-all(f32[32,16,256]{2,1,0:T(8,128)S(1)} %broadcast_in_dim.33), channel_id=1, replica_groups=mesh['rows_0'=8,'rows_1'=4,'rows_2'=2,'cols'=4] {'rows_0','rows_1'}, dimensions={0} | all-to-all | bytes 1048576 | tf_op jit(solution)/shard_map/all_to_all | solution.py:42
  69.7 7.8 %all_to_all.60 = f32[2,32,16,256]{3,2,1,0:T(8,128)S(1)} all-to-all(f32[2,32,16,256]{3,2,1,0:T(8,128)S(1)} %broadcast_in_dim.34), channel_id=1, replica_groups=mesh['rows_0'=8,'rows_1'=4,'rows_2'=2,'cols'=4] {'rows_2'}, dimensions={0} | all-to-all | bytes 2097152 | tf_op jit(solution)/shard_map/all_to_all | solution.py:42
  78.5 4.0 all-to-all-start.4
  83.2 19.1 %all-to-all-done.4 = f32[4,256,256]{2,1,0:T(8,128)S(1)} async-done(((f32[4,256,256]{2,1,0:T(8,128)}), f32[4,256,256]{2,1,0:T(8,128)S(1)}, u32[]{:S(2)}, u32[]{:S(2)}) %all-to-all-start.4) | async-done | bytes 1048608 | tf_op jit(solution)/shard_map/all_to_all | solution.py:81
  102.8 29.1 %all-gather.3.cloned.1.call-done = f32[1024,1024]{1,0:T(8,128)} async-done(((f32[1024,256]{1,0:T(8,128)}), f32[1024,1024]{1,0:T(8,128)}) %all-gather.3.cloned.1.call-update) | async-done | bytes 4194320 | tf_op jit(solution)/shard_map/all_gather | solution.py:82
  131.9 2.7 multiply_reduce_fusion
  135.4 14.4 %multiply_exponential_fusion = f32[1024,1024]{0,1:T(8,128)S(1)} fusion(f32[1024,1024]{1,0:T(8,128)S(1)} %copy-done.1, f32[1024]{0:T(1024)S(1)} %multiply_reduce_fusion), kind=kOutput, calls=%fused_computation.5 | convolution fusion | flops 12890144768 | bytes 8392704 | tf_op jit(solution)/shard_map/dot_general | solution.py:92
  149.8 2.0 copy-done.4
  152.2 1.4 fusion.6
  153.7 11.7 %cholesky.286 = f32[128,128]{1,0:T(8,128)S(1)} custom-call(f32[128,128]{1,0:T(8,128)S(1)} %cholesky.426), custom_call_target="Cholesky" | custom-call | tf_op jit(solution)/shard_map/jit(cholesky)/cholesky | solution.py:98
  165.5 9.8 %custom-call.31 = f32[1,128,128]{1,2,0:T(8,128)S(1)} custom-call(f32[1,128,128]{2,1,0:T(8,128)S(1)} %get-tuple-element.123), custom_call_target="InvertDiagBlocksLowerTriangular" | custom-call | tf_op jit(solution)/shard_map/jit(cholesky)/cholesky | solution.py:98
  176.8 12.1 %cholesky.305 = f32[128,128]{1,0:T(8,128)S(1)} custom-call(f32[128,128]{1,0:T(8,128)S(1)} %cholesky.430), custom_call_target="Cholesky" | custom-call | tf_op jit(solution)/shard_map/jit(cholesky)/cholesky | solution.py:98
  189.1 10.4 %custom-call.32 = f32[1,128,128]{1,2,0:T(8,128)} custom-call(f32[1,128,128]{2,1,0:T(8,128)S(1)} %get-tuple-element.121), custom_call_target="InvertDiagBlocksLowerTriangular" | custom-call | tf_op jit(solution)/shard_map/jit(cholesky)/cholesky | solution.py:98
  201.8 1.5 convolution_subtract_fusion.12
  203.3 11.7 %cholesky.326 = f32[128,128]{1,0:T(8,128)S(1)} custom-call(f32[128,128]{1,0:T(8,128)S(1)} %cholesky.435), custom_call_target="Cholesky" | custom-call | tf_op jit(solution)/shard_map/jit(cholesky)/cholesky | solution.py:98
  215.2 9.8 %custom-call.33 = f32[1,128,128]{1,2,0:T(8,128)S(1)} custom-call(f32[1,128,128]{2,1,0:T(8,128)S(1)} %get-tuple-element.119), custom_call_target="InvertDiagBlocksLowerTriangular" | custom-call | tf_op jit(solution)/shard_map/jit(cholesky)/cholesky | solution.py:98
  226.6 11.9 %cholesky.343 = f32[128,128]{1,0:T(8,128)S(1)} custom-call(f32[128,128]{1,0:T(8,128)S(1)} %convolution_subtract_fusion.16), custom_call_target="Cholesky" | custom-call | tf_op jit(solution)/shard_map/jit(cholesky)/cholesky | solution.py:98
  243.8 8.5 %while.5 = (s32[]{:T(128)}, f32[512,512]{0,1:T(8,128)S(1)}, s32[4,2]{0,1:T(2,128)S(1)}, f32[4,128,128]{2,1,0:T(8,128)S(1)}, s32[]{:T(128)}) while((s32[]{:T(128)}, f32[512,512]{0,1:T(8,128)S(1)}, s32[4,2]{0,1:T(2,128)S(1)}, f32[4,128,128]{2,1,0:T(8,128)S(1)}, s32[]{:T(128)}) %tuple.72), condition=%wide.while_cond, body=%wide.while_body.sunk | while | flops 2 | bytes 393329 | solution.py:66
  244.4 1.4 dynamic-slice.16
  252.3 39.3 %custom-call.34 = f32[4,128,128]{1,2,0:T(8,128)S(1)} custom-call(f32[4,128,128]{2,1,0:T(8,128)S(1)} %get-tuple-element.26), custom_call_target="InvertDiagBlocksLowerTriangular" | custom-call | tf_op jit(solution)/shard_map/triangular_solve/custom-call.3 | solution.py:66
  293.0 5.5 fusion.4
  301.1 1.4 convolution_subtract_fusion.3
  302.9 1.4 convolution_subtract_fusion.2
  304.8 1.6 convolution_subtract_fusion.4
  306.8 3.2 select_add_fusion
  310.0 2.6 convolution_subtract_fusion.1
  313.3 12.1 %cholesky.358 = f32[128,128]{1,0:T(8,128)S(1)} custom-call(f32[128,128]{1,0:T(8,128)S(1)} %cholesky.439), custom_call_target="Cholesky" | custom-call | tf_op jit(solution)/shard_map/jit(cholesky)/cholesky | solution.py:108
  326.1 9.8 %custom-call.35 = f32[1,128,128]{1,2,0:T(8,128)S(1)} custom-call(f32[1,128,128]{2,1,0:T(8,128)S(1)} %get-tuple-element.117), custom_call_target="InvertDiagBlocksLowerTriangular" | custom-call | tf_op jit(solution)/shard_map/jit(cholesky)/cholesky | solution.py:108
  336.7 11.7 %cholesky.377 = f32[128,128]{1,0:T(8,128)S(1)} custom-call(f32[128,128]{1,0:T(8,128)S(1)} %cholesky.443), custom_call_target="Cholesky" | custom-call | tf_op jit(solution)/shard_map/jit(cholesky)/cholesky | solution.py:108
  349.1 9.8 %custom-call.36 = f32[1,128,128]{1,2,0:T(8,128)S(1)} custom-call(f32[1,128,128]{2,1,0:T(8,128)S(1)} %get-tuple-element.114), custom_call_target="InvertDiagBlocksLowerTriangular" | custom-call | tf_op jit(solution)/shard_map/jit(cholesky)/cholesky | solution.py:108
  359.6 11.9 %cholesky.398 = f32[128,128]{1,0:T(8,128)S(1)} custom-call(f32[128,128]{1,0:T(8,128)S(1)} %cholesky.448), custom_call_target="Cholesky" | custom-call | tf_op jit(solution)/shard_map/jit(cholesky)/cholesky | solution.py:108
  372.1 9.8 %custom-call.37 = f32[1,128,128]{1,2,0:T(8,128)S(1)} custom-call(f32[1,128,128]{2,1,0:T(8,128)S(1)} %get-tuple-element.111), custom_call_target="InvertDiagBlocksLowerTriangular" | custom-call | tf_op jit(solution)/shard_map/jit(cholesky)/cholesky | solution.py:108
  382.6 11.7 %cholesky.415 = f32[128,128]{1,0:T(8,128)S(1)} custom-call(f32[128,128]{1,0:T(8,128)S(1)} %convolution_subtract_fusion.15), custom_call_target="Cholesky" | custom-call | tf_op jit(solution)/shard_map/jit(cholesky)/cholesky | solution.py:108
  397.7 8.1 %while.6 = (s32[]{:T(128)}, f32[512,512]{1,0:T(8,128)S(1)}, s32[4,2]{0,1:T(2,128)S(1)}, f32[4,128,128]{2,1,0:T(8,128)S(1)}, s32[]{:T(128)}) while((s32[]{:T(128)}, f32[512,512]{1,0:T(8,128)S(1)}, s32[4,2]{0,1:T(2,128)S(1)}, f32[4,128,128]{2,1,0:T(8,128)S(1)}, s32[]{:T(128)}) %tuple.82), condition=%wide.while_cond.clone, body=%wide.while_body.clone.sunk | while | flops 2 | bytes 131189 | solution.py:66
  405.8 39.5 %custom-call.38 = f32[4,128,128]{1,2,0:T(8,128)S(1)} custom-call(f32[4,128,128]{2,1,0:T(8,128)S(1)} %get-tuple-element.27), custom_call_target="InvertDiagBlocksLowerTriangular" | custom-call | tf_op jit(solution)/shard_map/triangular_solve/custom-call.3 | solution.py:66
  452.3 45.2 %all-gather.5.cloned.1.call-done = f32[1024,1024]{0,1:T(8,128)} async-done(((f32[256,1024]{0,1:T(8,128)}), f32[1024,1024]{0,1:T(8,128)}) %all-gather.5.cloned.1.call-update) | async-done | bytes 4194320 | tf_op jit(solution)/shard_map/all_gather | solution.py:113
  497.5 5.2 fusion.98
  503.1 4.3 all_to_all.61
  508.0 1.5 reduce.17
  510.0 18.7 %all_to_all.64 = f32[32,1,1024]{2,1,0:T(1,128)S(1)} all-to-all(f32[32,1,1024]{2,1,0:T(1,128)S(1)} %reshape.232), channel_id=1, replica_groups=mesh['rows_0'=8,'rows_1'=4,'rows_2'=2,'cols'=4] {'rows_0','rows_1'}, dimensions={0} | all-to-all | bytes 262144 | tf_op jit(solution)/shard_map/all_to_all | solution.py:29
  530.8 3.9 all-to-all-start.7
  536.0 8.0 %all-to-all-done.7 = f32[32,1,1024]{2,1,0:T(1,128)S(1)} async-done(((f32[32,1,1024]{2,1,0:T(1,128)}), f32[32,1,1024]{2,1,0:T(1,128)S(1)}, u32[]{:S(2)}, u32[]{:S(2)}) %all-to-all-start.7) | async-done | bytes 131104 | tf_op jit(solution)/shard_map/all_to_all | solution.py:42
  545.5 6.9 %all_to_all.62 = f32[2,1,32768]{2,1,0:T(1,128)S(1)} all-to-all(f32[2,1,32768]{2,1,0:T(1,128)S(1)} %reshape.236), channel_id=1, replica_groups=mesh['rows_0'=8,'rows_1'=4,'rows_2'=2,'cols'=4] {'rows_2'}, dimensions={0} | all-to-all | bytes 524288 | tf_op jit(solution)/shard_map/all_to_all | solution.py:42
  552.4 1.5 reduce.20
  (165 shorter events, 55.4 us)
Async XLA Ops:
  7.2 490.3 %copy-start = (f32[1024,64]{0,1:T(8,128)S(1)}, f32[1024,64]{0,1:T(8,128)}, u32[]{:S(2)}) copy-start(f32[1024,64]{0,1:T(8,128)} %param.8) | copy-start | bytes 786436
  14.8 8.6 %all-to-all-start = ((f32[2,32,16,256]{3,2,1,0:T(8,128)}), f32[2,32,16,256]{3,2,1,0:T(8,128)S(1)}, u32[]{:S(2)}, u32[]{:S(2)}) async-start(f32[2,32,16,256]{3,2,1,0:T(8,128)} %fusion.7), calls=%async_computation | async-start | bytes 2097152 | tf_op jit(solution)/shard_map/all_to_all | solution.py:21
  21.6 110.3 %all-gather.3.cloned.1.call-start = ((), (), s32[]{:S(2)}) async-start(), calls=%async_computation.9 | async-start | bytes 5242880 | tf_op jit(solution)/shard_map/all_gather | solution.py:82
  78.5 23.8 %all-to-all-start.4 = ((f32[4,256,256]{2,1,0:T(8,128)}), f32[4,256,256]{2,1,0:T(8,128)S(1)}, u32[]{:S(2)}, u32[]{:S(2)}) async-start(f32[4,256,256]{2,1,0:T(8,128)} %bitcast.13), calls=%async_computation.4 | async-start | bytes 2097152 | tf_op jit(solution)/shard_map/all_to_all | solution.py:81
  82.5 415.0 %all-gather.5.cloned.1.call-start = ((), (), s32[]{:S(2)}) async-start(), calls=%async_computation.10 | async-start | bytes 5242880 | tf_op jit(solution)/shard_map/all_gather | solution.py:113
  131.9 3.4 copy-start.1
  149.8 2.0 copy-start.4
  153.6 35.4 %copy-start.3 = (f32[512,512]{1,0:T(8,128)}, f32[512,512]{1,0:T(8,128)S(1)}, u32[]{:S(2)}) copy-start(f32[512,512]{1,0:T(8,128)S(1)} %fusion.6) | copy-start | bytes 3145732
  176.0 13.1 %copy-start.9 = (f32[384,128]{1,0:T(8,128)}, f32[384,128]{1,0:T(8,128)S(1)}, u32[]{:S(2)}) copy-start(f32[384,128]{1,0:T(8,128)S(1)} %convolution_subtract_fusion.6) | copy-start | bytes 589828
  299.5 10.5 %copy-start.5 = (f32[256,128]{0,1:T(8,128)}, f32[256,128]{0,1:T(8,128)S(1)}, u32[]{:S(2)}) copy-start(f32[256,128]{0,1:T(8,128)S(1)} %fusion.78) | copy-start | bytes 393220
  300.2 9.8 %copy-start.7 = (f32[256,128]{0,1:T(8,128)}, f32[256,128]{0,1:T(8,128)S(1)}, u32[]{:S(2)}) copy-start(f32[256,128]{0,1:T(8,128)S(1)} %fusion.80) | copy-start | bytes 393220
  301.1 9.0 %copy-start.10 = (f32[256,128]{0,1:T(8,128)}, f32[256,128]{0,1:T(8,128)S(1)}, u32[]{:S(2)}) copy-start(f32[256,128]{0,1:T(8,128)S(1)} %fusion.82) | copy-start | bytes 393220
  358.9 92.3 %copy-start.6 = (f32[256,128]{0,1:T(8,128)S(1)}, f32[256,128]{0,1:T(8,128)}, u32[]{:S(2)}) copy-start(f32[256,128]{0,1:T(8,128)} %copy-done.5) | copy-start | bytes 393220
  358.9 92.3 %copy-start.8 = (f32[256,128]{0,1:T(8,128)S(1)}, f32[256,128]{0,1:T(8,128)}, u32[]{:S(2)}) copy-start(f32[256,128]{0,1:T(8,128)} %copy-done.7) | copy-start | bytes 393220
  358.9 92.3 %copy-start.11 = (f32[256,128]{0,1:T(8,128)S(1)}, f32[256,128]{0,1:T(8,128)}, u32[]{:S(2)}) copy-start(f32[256,128]{0,1:T(8,128)} %copy-done.10) | copy-start | bytes 393220
  502.7 32.0 %copy-start.2 = (f32[256,1024]{0,1:T(8,128)S(1)}, f32[256,1024]{0,1:T(8,128)}, u32[]{:S(2)}) copy-start(f32[256,1024]{0,1:T(8,128)} %maximum_maximum_fusion) | copy-start | bytes 3145732
  530.8 13.2 %all-to-all-start.7 = ((f32[32,1,1024]{2,1,0:T(1,128)}), f32[32,1,1024]{2,1,0:T(1,128)S(1)}, u32[]{:S(2)}, u32[]{:S(2)}) async-start(f32[32,1,1024]{2,1,0:T(1,128)} %reshape.234), calls=%async_computation.7 | async-start | bytes 262144 | tf_op jit(solution)/shard_map/all_to_all | solution.py:42
Sparse Core Ops, SparseCore 0:
  78.6 53.2 all-gather.2
  452.4 45.0 all-gather.4
where the time goes:
time: 566 us; the launch traced here: 562 us
  other arithmetic  251 us (44%)
  waiting for transfers between devices  103 us (18%)
  blocking collectives  83.6 us (15%)
  matrix products  53.2 us (9%)
  local copies, waits for them, and re-layouts  36.3 us (6%)
  between operations  20.1 us (4%)
  starting transfers between devices  14.9 us (3%)
    another operation x15, other arithmetic, shards(): low_two = jnp.linalg.cholesky(schur + RIDGE * identity)  79.6 us
    another operation x5, other arithmetic, right_side_solve(): lax.linalg.triangular_solve(low, values, left_side=False, lower=True, tra...  79.6 us
    another operation x14, other arithmetic, shards(): low_one = jnp.linalg.cholesky(pivot_kern[:block, :block] + RIDGE * identity)  79.5 us
    all_gather x1, waiting for transfers between devices, shards(): lax.all_gather(factor, 'cols', axis=0, tiled=True)  45.2 us
    all_to_all x2, blocking collectives, sum_by_axis(): lax.all_to_all(nearer, far, split_axis=0, concat_axis=0, tiled=True)  44.6 us
    all_to_all x3, blocking collectives, copy_for_each(): return lax.all_to_all(copies, axis, split_axis=0, concat_axis=0, tiled=True)  34.7 us
    all_gather x1, waiting for transfers between devices, shards(): pivot_full = lax.all_gather(pivot_part, 'cols', axis=1, tiled=True)  29.1 us
    all_to_all x1, waiting for transfers between devices, shards(): lax.all_to_all(points, 'cols', split_axis=0, concat_axis=1, tiled=True)  19.1 us
  transfers between devices with their start and end apart: 5, of which 5 were waited for; matrix products, arithmetic and copies ran while one was open for 0% of the time, Pallas kernels for 0%

commit v1 on v0

--- a/solution.py
+++ b/solution.py
@@ -78,7 +78,10 @@
     mine = owner == row_me
     picked = jnp.where(mine[:, None], points[inside], 0.0)
     pivot_part = sum_by_parts(picked, (("rows_0", "rows_1"), "rows_2"))
-    own_rows = lax.all_to_all(points, "cols", split_axis=0, concat_axis=1, tiled=True)
+    size = lax.axis_size("cols")
+    pieces = jnp.stack(jnp.split(points, size, axis=0), axis=0)
+    pieces = lax.all_to_all(pieces, "cols", split_axis=0, concat_axis=0)
+    own_rows = jnp.concatenate(pieces, axis=1)
     pivot_full = lax.all_gather(pivot_part, "cols", axis=1, tiled=True)
     own_norms = jnp.sum(own_rows * own_rows, axis=1)
     full_norms = jnp.sum(pivot_full * pivot_full, axis=1)

time: 566 us -> 573 us (1.012)
  transfers between devices with their start and end apart: 5 -> 5, of which waited for: 5 -> 5; matrix products, arithmetic and copies ran while one was open for 0% -> 1% of each run, Pallas kernels for 0% -> 0%
where the time goes in v1:
time: 573 us; the launch traced here: 569 us
  other arithmetic  252 us (44%)
  waiting for transfers between devices  103 us (18%)
  blocking collectives  83.7 us (15%)
  matrix products  58.2 us (10%)
  local copies, waits for them, and re-layouts  36.6 us (6%)
  between operations  20.4 us (4%)
  starting transfers between devices  14.9 us (3%)
    another operation x5, other arithmetic, right_side_solve(): lax.linalg.triangular_solve(low, values, left_side=False, lower=True, tra...  79.7 us
    another operation x15, other arithmetic, shards(): low_two = jnp.linalg.cholesky(schur + RIDGE * identity)  79.4 us
    another operation x14, other arithmetic, shards(): low_one = jnp.linalg.cholesky(pivot_kern[:block, :block] + RIDGE * identity)  79.3 us
    all_gather x1, waiting for transfers between devices, shards(): lax.all_gather(factor, 'cols', axis=0, tiled=True)  45.2 us
    all_to_all x2, blocking collectives, sum_by_axis(): lax.all_to_all(nearer, far, split_axis=0, concat_axis=0, tiled=True)  44.6 us
    all_to_all x3, blocking collectives, copy_for_each(): return lax.all_to_all(copies, axis, split_axis=0, concat_axis=0, tiled=True)  34.9 us
    all_gather x1, waiting for transfers between devices, shards(): pivot_full = lax.all_gather(pivot_part, 'cols', axis=1, tiled=True)  27.7 us
    all_to_all x1, waiting for transfers between devices, shards(): pieces = lax.all_to_all(pieces, 'cols', split_axis=0, concat_axis=0)  20.7 us
  transfers between devices with their start and end apart: 5, of which 5 were waited for; matrix products, arithmetic and copies ran while one was open for 1% of the time, Pallas kernels for 0%

profile of v1, /device:TPU:1, one launch (start us, length us, event | category | flops | bytes accessed | tf_op | source)
XLA Modules:
  0.0 569.0 jit_solution(16793298776348316458)
XLA Ops:
  9.0 4.7 gather_fusion
  14.8 6.8 %all-to-all-start = ((f32[2,32,16,256]{3,2,1,0:T(8,128)}), f32[2,32,16,256]{3,2,1,0:T(8,128)S(1)}, u32[]{:S(2)}, u32[]{:S(2)}) async-start(f32[2,32,16,256]{3,2,1,0:T(8,128)} %fusion.7), calls=%async_computation | async-start | bytes 2097152 | tf_op jit(solution)/shard_map/all_to_all | solution.py:21
  21.6 1.7 all-to-all-done
  23.5 25.9 %all_to_all.49 = f32[32,16,256]{2,1,0:T(8,128)S(1)} all-to-all(f32[32,16,256]{2,1,0:T(8,128)S(1)} %reduce_sum.58), channel_id=1, replica_groups=mesh['rows_0'=8,'rows_1'=4,'rows_2'=2,'cols'=4] {'rows_0','rows_1'}, dimensions={0} | all-to-all | bytes 1048576 | tf_op jit(solution)/shard_map/all_to_all | solution.py:29
  49.5 20.2 %all_to_all.45 = f32[32,16,256]{2,1,0:T(8,128)S(1)} all-to-all(f32[32,16,256]{2,1,0:T(8,128)S(1)} %broadcast_in_dim.33), channel_id=1, replica_groups=mesh['rows_0'=8,'rows_1'=4,'rows_2'=2,'cols'=4] {'rows_0','rows_1'}, dimensions={0} | all-to-all | bytes 1048576 | tf_op jit(solution)/shard_map/all_to_all | solution.py:42
  69.8 7.8 %all_to_all.46 = f32[2,32,16,256]{3,2,1,0:T(8,128)S(1)} all-to-all(f32[2,32,16,256]{3,2,1,0:T(8,128)S(1)} %broadcast_in_dim.34), channel_id=1, replica_groups=mesh['rows_0'=8,'rows_1'=4,'rows_2'=2,'cols'=4] {'rows_2'}, dimensions={0} | all-to-all | bytes 2097152 | tf_op jit(solution)/shard_map/all_to_all | solution.py:42
  80.3 4.0 all-to-all-start.4
  85.1 20.7 %all-to-all-done.4 = f32[4,256,256]{1,2,0:T(8,128)S(1)} async-done(((f32[4,256,256]{1,2,0:T(8,128)}), f32[4,256,256]{1,2,0:T(8,128)S(1)}, u32[]{:S(2)}, u32[]{:S(2)}) %all-to-all-start.4) | async-done | bytes 1048608 | tf_op jit(solution)/shard_map/all_to_all | solution.py:83
  106.0 27.7 %all-gather.3.cloned.1.call-done = f32[1024,1024]{1,0:T(8,128)} async-done(((f32[1024,256]{1,0:T(8,128)}), f32[1024,1024]{1,0:T(8,128)}) %all-gather.3.cloned.1.call-update) | async-done | bytes 4194320 | tf_op jit(solution)/shard_map/all_gather | solution.py:85
  133.7 2.7 multiply_reduce_fusion
  137.2 14.6 %multiply_exponential_fusion = f32[1024,1024]{0,1:T(8,128)S(1)} fusion(f32[1024,1024]{1,0:T(8,128)S(1)} %copy-done.2, f32[1024]{0:T(1024)S(1)} %multiply_reduce_fusion), kind=kOutput, calls=%fused_computation.5 | convolution fusion | flops 12890144768 | bytes 8392704 | tf_op jit(solution)/shard_map/dot_general | solution.py:95
  151.8 2.0 copy-done.5
  154.2 1.4 fusion.6
  155.7 11.7 %cholesky.286 = f32[128,128]{1,0:T(8,128)S(1)} custom-call(f32[128,128]{1,0:T(8,128)S(1)} %cholesky.426), custom_call_target="Cholesky" | custom-call | tf_op jit(solution)/shard_map/jit(cholesky)/cholesky | solution.py:101
  167.5 9.8 %custom-call.31 = f32[1,128,128]{1,2,0:T(8,128)S(1)} custom-call(f32[1,128,128]{2,1,0:T(8,128)S(1)} %get-tuple-element.117), custom_call_target="InvertDiagBlocksLowerTriangular" | custom-call | tf_op jit(solution)/shard_map/jit(cholesky)/cholesky | solution.py:101
  178.8 11.9 %cholesky.305 = f32[128,128]{1,0:T(8,128)S(1)} custom-call(f32[128,128]{1,0:T(8,128)S(1)} %cholesky.430), custom_call_target="Cholesky" | custom-call | tf_op jit(solution)/shard_map/jit(cholesky)/cholesky | solution.py:101
  190.9 10.4 %custom-call.32 = f32[1,128,128]{1,2,0:T(8,128)} custom-call(f32[1,128,128]{2,1,0:T(8,128)S(1)} %get-tuple-element.115), custom_call_target="InvertDiagBlocksLowerTriangular" | custom-call | tf_op jit(solution)/shard_map/jit(cholesky)/cholesky | solution.py:101
  203.6 1.5 convolution_subtract_fusion.12
  205.1 11.7 %cholesky.326 = f32[128,128]{1,0:T(8,128)S(1)} custom-call(f32[128,128]{1,0:T(8,128)S(1)} %cholesky.435), custom_call_target="Cholesky" | custom-call | tf_op jit(solution)/shard_map/jit(cholesky)/cholesky | solution.py:101
  217.0 9.8 %custom-call.33 = f32[1,128,128]{1,2,0:T(8,128)S(1)} custom-call(f32[1,128,128]{2,1,0:T(8,128)S(1)} %get-tuple-element.113), custom_call_target="InvertDiagBlocksLowerTriangular" | custom-call | tf_op jit(solution)/shard_map/jit(cholesky)/cholesky | solution.py:101
  228.4 11.9 %cholesky.343 = f32[128,128]{1,0:T(8,128)S(1)} custom-call(f32[128,128]{1,0:T(8,128)S(1)} %convolution_subtract_fusion.16), custom_call_target="Cholesky" | custom-call | tf_op jit(solution)/shard_map/jit(cholesky)/cholesky | solution.py:101
  245.7 8.5 %while.5 = (s32[]{:T(128)}, f32[512,512]{0,1:T(8,128)S(1)}, s32[4,2]{0,1:T(2,128)S(1)}, f32[4,128,128]{2,1,0:T(8,128)S(1)}, s32[]{:T(128)}) while((s32[]{:T(128)}, f32[512,512]{0,1:T(8,128)S(1)}, s32[4,2]{0,1:T(2,128)S(1)}, f32[4,128,128]{2,1,0:T(8,128)S(1)}, s32[]{:T(128)}) %tuple.72), condition=%wide.while_cond, body=%wide.while_body.sunk | while | flops 2 | bytes 393329 | solution.py:66
  254.1 39.3 %custom-call.34 = f32[4,128,128]{1,2,0:T(8,128)S(1)} custom-call(f32[4,128,128]{2,1,0:T(8,128)S(1)} %get-tuple-element.26), custom_call_target="InvertDiagBlocksLowerTriangular" | custom-call | tf_op jit(solution)/shard_map/triangular_solve/custom-call.3 | solution.py:66
  294.8 9.7 %fusion.3 = f32[256,1024]{1,0:T(8,128)S(1)} fusion(f32[256,1024]{0,1:T(8,128)S(1)} %bitcast.144, f32[1024,1024]{1,0:T(8,128)} %all-gather.3.cloned.1.call-done, f32[1024]{0:T(1024)S(1)} %multiply_reduce_fusion, f32[256]{0:T(256)S(1)} %fusion.5), kind=kOutput, calls=%fused_computation.14 | convolution fusion | flops 3222536192 | bytes 6296576 | tf_op jit(solution)/shard_map/dot_general | solution.py:88
  309.5 1.4 convolution_subtract_fusion.2
  311.3 1.6 convolution_subtract_fusion.4
  313.4 3.2 select_add_fusion
  316.6 1.9 convolution_subtract_fusion.1
  319.1 11.9 %cholesky.358 = f32[128,128]{1,0:T(8,128)S(1)} custom-call(f32[128,128]{1,0:T(8,128)S(1)} %cholesky.439), custom_call_target="Cholesky" | custom-call | tf_op jit(solution)/shard_map/jit(cholesky)/cholesky | solution.py:111
  331.7 9.8 %custom-call.35 = f32[1,128,128]{1,2,0:T(8,128)S(1)} custom-call(f32[1,128,128]{2,1,0:T(8,128)S(1)} %get-tuple-element.111), custom_call_target="InvertDiagBlocksLowerTriangular" | custom-call | tf_op jit(solution)/shard_map/jit(cholesky)/cholesky | solution.py:111
  342.3 11.7 %cholesky.377 = f32[128,128]{1,0:T(8,128)S(1)} custom-call(f32[128,128]{1,0:T(8,128)S(1)} %cholesky.443), custom_call_target="Cholesky" | custom-call | tf_op jit(solution)/shard_map/jit(cholesky)/cholesky | solution.py:111
  354.7 9.8 %custom-call.36 = f32[1,128,128]{1,2,0:T(8,128)S(1)} custom-call(f32[1,128,128]{2,1,0:T(8,128)S(1)} %get-tuple-element.108), custom_call_target="InvertDiagBlocksLowerTriangular" | custom-call | tf_op jit(solution)/shard_map/jit(cholesky)/cholesky | solution.py:111
  365.3 11.9 %cholesky.398 = f32[128,128]{1,0:T(8,128)S(1)} custom-call(f32[128,128]{1,0:T(8,128)S(1)} %cholesky.448), custom_call_target="Cholesky" | custom-call | tf_op jit(solution)/shard_map/jit(cholesky)/cholesky | solution.py:111
  377.8 9.8 %custom-call.37 = f32[1,128,128]{1,2,0:T(8,128)S(1)} custom-call(f32[1,128,128]{2,1,0:T(8,128)S(1)} %get-tuple-element.105), custom_call_target="InvertDiagBlocksLowerTriangular" | custom-call | tf_op jit(solution)/shard_map/jit(cholesky)/cholesky | solution.py:111
  388.2 11.7 %cholesky.415 = f32[128,128]{1,0:T(8,128)S(1)} custom-call(f32[128,128]{1,0:T(8,128)S(1)} %convolution_subtract_fusion.15), custom_call_target="Cholesky" | custom-call | tf_op jit(solution)/shard_map/jit(cholesky)/cholesky | solution.py:111
  403.3 8.1 %while.6 = (s32[]{:T(128)}, f32[512,512]{1,0:T(8,128)S(1)}, s32[4,2]{0,1:T(2,128)S(1)}, f32[4,128,128]{2,1,0:T(8,128)S(1)}, s32[]{:T(128)}) while((s32[]{:T(128)}, f32[512,512]{1,0:T(8,128)S(1)}, s32[4,2]{0,1:T(2,128)S(1)}, f32[4,128,128]{2,1,0:T(8,128)S(1)}, s32[]{:T(128)}) %tuple.82), condition=%wide.while_cond.clone, body=%wide.while_body.clone.sunk | while | flops 2 | bytes 131189 | solution.py:66
  411.4 39.6 %custom-call.38 = f32[4,128,128]{1,2,0:T(8,128)S(1)} custom-call(f32[4,128,128]{2,1,0:T(8,128)S(1)} %get-tuple-element.27), custom_call_target="InvertDiagBlocksLowerTriangular" | custom-call | tf_op jit(solution)/shard_map/triangular_solve/custom-call.3 | solution.py:66
  453.9 1.5 convolution_subtract_fusion.8
  455.7 1.7 convolution_subtract_fusion.7
  458.9 45.2 %all-gather.5.cloned.1.call-done = f32[1024,1024]{0,1:T(8,128)} async-done(((f32[256,1024]{0,1:T(8,128)}), f32[1024,1024]{0,1:T(8,128)}) %all-gather.5.cloned.1.call-update) | async-done | bytes 4194320 | tf_op jit(solution)/shard_map/all_gather | solution.py:116
  504.0 5.2 fusion.99
  509.6 4.3 all_to_all.47
  514.5 1.5 reduce.17
  516.6 18.7 %all_to_all.50 = f32[32,1,1024]{2,1,0:T(1,128)S(1)} all-to-all(f32[32,1,1024]{2,1,0:T(1,128)S(1)} %reshape.237), channel_id=1, replica_groups=mesh['rows_0'=8,'rows_1'=4,'rows_2'=2,'cols'=4] {'rows_0','rows_1'}, dimensions={0} | all-to-all | bytes 262144 | tf_op jit(solution)/shard_map/all_to_all | solution.py:29
  537.3 3.9 all-to-all-start.7
  542.5 8.0 %all-to-all-done.7 = f32[32,1,1024]{2,1,0:T(1,128)S(1)} async-done(((f32[32,1,1024]{2,1,0:T(1,128)}), f32[32,1,1024]{2,1,0:T(1,128)S(1)}, u32[]{:S(2)}, u32[]{:S(2)}) %all-to-all-start.7) | async-done | bytes 131104 | tf_op jit(solution)/shard_map/all_to_all | solution.py:42
  552.0 6.9 %all_to_all.48 = f32[2,1,32768]{2,1,0:T(1,128)S(1)} all-to-all(f32[2,1,32768]{2,1,0:T(1,128)S(1)} %reshape.241), channel_id=1, replica_groups=mesh['rows_0'=8,'rows_1'=4,'rows_2'=2,'cols'=4] {'rows_2'}, dimensions={0} | all-to-all | bytes 524288 | tf_op jit(solution)/shard_map/all_to_all | solution.py:42
  558.9 1.5 reduce.20
  (172 shorter events, 57.8 us)
Async XLA Ops:
  7.2 496.9 %copy-start = (f32[1024,64]{0,1:T(8,128)S(1)}, f32[1024,64]{0,1:T(8,128)}, u32[]{:S(2)}) copy-start(f32[1024,64]{0,1:T(8,128)} %param.8) | copy-start | bytes 786436
  14.8 8.6 %all-to-all-start = ((f32[2,32,16,256]{3,2,1,0:T(8,128)}), f32[2,32,16,256]{3,2,1,0:T(8,128)S(1)}, u32[]{:S(2)}, u32[]{:S(2)}) async-start(f32[2,32,16,256]{3,2,1,0:T(8,128)} %fusion.7), calls=%async_computation | async-start | bytes 2097152 | tf_op jit(solution)/shard_map/all_to_all | solution.py:21
  21.6 112.1 %all-gather.3.cloned.1.call-start = ((), (), s32[]{:S(2)}) async-start(), calls=%async_computation.9 | async-start | bytes 5242880 | tf_op jit(solution)/shard_map/all_gather | solution.py:85
  49.4 29.3 %copy-start.1 = (f32[1024,256]{1,0:T(8,128)S(1)}, f32[1024,256]{1,0:T(8,128)}, u32[]{:S(2)}) copy-start(f32[1024,256]{1,0:T(8,128)} %param.6) | copy-start | bytes 3145732
  80.3 25.5 %all-to-all-start.4 = ((f32[4,256,256]{1,2,0:T(8,128)}), f32[4,256,256]{1,2,0:T(8,128)S(1)}, u32[]{:S(2)}, u32[]{:S(2)}) async-start(f32[4,256,256]{1,2,0:T(8,128)} %pad_maximum_fusion), calls=%async_computation.4 | async-start | bytes 2097152 | tf_op jit(solution)/shard_map/all_to_all | solution.py:83
  84.4 419.7 %all-gather.5.cloned.1.call-start = ((), (), s32[]{:S(2)}) async-start(), calls=%async_computation.10 | async-start | bytes 5242880 | tf_op jit(solution)/shard_map/all_gather | solution.py:116
  133.7 3.4 copy-start.2
  151.8 2.0 copy-start.5
  155.7 35.2 %copy-start.4 = (f32[512,512]{1,0:T(8,128)}, f32[512,512]{1,0:T(8,128)S(1)}, u32[]{:S(2)}) copy-start(f32[512,512]{1,0:T(8,128)S(1)} %fusion.6) | copy-start | bytes 3145732
  178.0 12.8 %copy-start.10 = (f32[384,128]{1,0:T(8,128)}, f32[384,128]{1,0:T(8,128)S(1)}, u32[]{:S(2)}) copy-start(f32[384,128]{1,0:T(8,128)S(1)} %convolution_subtract_fusion.6) | copy-start | bytes 589828
  305.5 11.0 %copy-start.6 = (f32[256,128]{0,1:T(8,128)}, f32[256,128]{0,1:T(8,128)S(1)}, u32[]{:S(2)}) copy-start(f32[256,128]{0,1:T(8,128)S(1)} %fusion.78) | copy-start | bytes 393220
  306.5 10.1 %copy-start.8 = (f32[256,128]{0,1:T(8,128)}, f32[256,128]{0,1:T(8,128)S(1)}, u32[]{:S(2)}) copy-start(f32[256,128]{0,1:T(8,128)S(1)} %fusion.80) | copy-start | bytes 393220
  307.6 9.0 %copy-start.11 = (f32[256,128]{0,1:T(8,128)}, f32[256,128]{0,1:T(8,128)S(1)}, u32[]{:S(2)}) copy-start(f32[256,128]{0,1:T(8,128)S(1)} %fusion.82) | copy-start | bytes 393220
  364.6 93.2 %copy-start.7 = (f32[256,128]{0,1:T(8,128)S(1)}, f32[256,128]{0,1:T(8,128)}, u32[]{:S(2)}) copy-start(f32[256,128]{0,1:T(8,128)} %copy-done.6) | copy-start | bytes 393220
  364.6 93.2 %copy-start.9 = (f32[256,128]{0,1:T(8,128)S(1)}, f32[256,128]{0,1:T(8,128)}, u32[]{:S(2)}) copy-start(f32[256,128]{0,1:T(8,128)} %copy-done.8) | copy-start | bytes 393220
  364.6 93.2 %copy-start.12 = (f32[256,128]{0,1:T(8,128)S(1)}, f32[256,128]{0,1:T(8,128)}, u32[]{:S(2)}) copy-start(f32[256,128]{0,1:T(8,128)} %copy-done.11) | copy-start | bytes 393220
  509.2 32.0 %copy-start.3 = (f32[256,1024]{0,1:T(8,128)S(1)}, f32[256,1024]{0,1:T(8,128)}, u32[]{:S(2)}) copy-start(f32[256,1024]{0,1:T(8,128)} %maximum_maximum_fusion) | copy-start | bytes 3145732
  537.3 13.2 %all-to-all-start.7 = ((f32[32,1,1024]{2,1,0:T(1,128)}), f32[32,1,1024]{2,1,0:T(1,128)S(1)}, u32[]{:S(2)}, u32[]{:S(2)}) async-start(f32[32,1,1024]{2,1,0:T(1,128)} %reshape.239), calls=%async_computation.7 | async-start | bytes 262144 | tf_op jit(solution)/shard_map/all_to_all | solution.py:42
Sparse Core Ops, SparseCore 0:
  78.8 54.9 all-gather.2
  459.0 45.0 all-gather.4
